TPU v7x, 256 devices: a whole 4x4x8 slice. The times are simulated.
256 devices in a mesh: chan: 64 (over x, z_hi, y, core), slab: 4 (over z_lo).
Axes of the slice: x: 4, y: 4, z: 8 (z_hi: 2, z_lo: 4; z = z_hi * 4 + z_lo), core: 2. Of those that a mesh axis runs over, the one named last changes fastest.
Arguments:
- activations: bfloat16 [128, 8, 64, 128], P('chan', 'slab'), may hold values from -6 to 6
- cotangent: bfloat16 [128, 8, 64, 128], P('chan', 'slab'), may hold values from -6 to 6
- relu_mask: int32 [128, 8, 64, 128], P('chan', 'slab'), may hold values 0 or 1
- weights: bfloat16 [3, 3, 3, 128, 128], replicated, may hold values from -0.109375 to 0.109375
Outputs:
- pre: bfloat16 [128, 8, 64, 128], P('chan', 'slab')
- grad_input: bfloat16 [128, 8, 64, 128], P('chan', 'slab')
All inputs are finite; a program needn't handle non-finite values. No bound on the sum of `relu_mask` on one device may be relied on, other than what follows from the above.
Results may differ from a plain program's by a relative error of at most 0.0013.
Values may be sent and summed in bfloat16 or wider, within the bound.
A program may use at most 64 MiB of HBM per device.

v0:
```python
import jax
import jax.numpy as jnp
from jax import lax
from jax.sharding import PartitionSpec as P


def with_halo(shard, sides, width):
    for axis, dim in sides:
        devices, length = (lax.axis_size(axis), shard.shape[dim])
        up = [(i, (i + 1) % devices) for i in range(devices - 1)]
        down = [(j, i) for i, j in up]
        last = lax.slice_in_dim(shard, length - width, length, axis=dim)
        first = lax.slice_in_dim(shard, 0, width, axis=dim)
        before = lax.ppermute(last, axis, up)
        after = lax.ppermute(first, axis, down)
        shard = jnp.concatenate([before, shard, after], axis=dim)
    return shard


def offset_list():
    return [(i, j, k) for i in range(3) for j in range(3) for k in range(3)]


def tap_windows(padded, planes, height, breadth, flipped):
    pieces = []
    for i, j, k in offset_list():
        if flipped:
            pieces.append(
                padded[:, 2 - i : 2 - i + planes, 2 - j : 2 - j + height, 2 - k : 2 - k + breadth]
            )
        else:
            pieces.append(padded[:, i : i + planes, j : j + height, k : k + breadth])
    return pieces


def forward_sum(w_rows, padded, planes, height, breadth):
    windows = tap_windows(padded, planes, height, breadth, False)
    total = jnp.zeros((w_rows.shape[3], planes, height, breadth), jnp.float32)
    for tap, (i, j, k) in enumerate(offset_list()):
        total = total + jnp.einsum(
            "oi,idhw->odhw", w_rows[i, j, k], windows[tap], preferred_element_type=jnp.float32
        )
    return total


def backward_sum(w_cols, padded, planes, height, breadth):
    outputs = w_cols.shape[4]
    windows = tap_windows(padded, planes, height, breadth, True)
    total = jnp.zeros((outputs, planes, height, breadth), jnp.float32)
    for tap, (i, j, k) in enumerate(offset_list()):
        total = total + jnp.einsum(
            "oi,odhw->idhw", w_cols[i, j, k], windows[tap], preferred_element_type=jnp.float32
        )
    return total


def body(activations, cotangent, relu_mask, weights):
    planes = activations.shape[1]
    breadth = activations.shape[3]
    masked = jnp.where(relu_mask == 1, cotangent, jnp.zeros_like(cotangent))
    stacked = jnp.stack([activations, masked])
    patches = lax.all_to_all(stacked, "chan", split_axis=3, concat_axis=1, tiled=True)
    rimmed = with_halo(patches, (("chan", 3), ("slab", 2)), 1)
    padded = jnp.pad(rimmed, ((0, 0), (0, 0), (0, 0), (0, 0), (1, 1)))
    row_block = patches.shape[3]
    pre_block = forward_sum(weights, padded[0], planes, row_block, breadth).astype(jnp.bfloat16)
    grad_block = backward_sum(weights, padded[1], planes, row_block, breadth).astype(jnp.bfloat16)
    pre, grad_input = (
        lax.all_to_all(pre_block, "chan", split_axis=0, concat_axis=2, tiled=True),
        lax.all_to_all(grad_block, "chan", split_axis=0, concat_axis=2, tiled=True),
    )
    return (pre, grad_input)


def solution(mesh):
    placed = (
        P("chan", "slab", None, None),
        P("chan", "slab", None, None),
        P("chan", "slab", None, None),
        P(),
    )
    return jax.shard_map(
        body,
        mesh=mesh,
        in_specs=placed,
        out_specs=(P("chan", "slab", None, None), P("chan", "slab", None, None)),
        check_vma=False,
    )
```

profile of v0, /device:TPU:1, one launch (start us, length us, event | category | flops | bytes accessed | tf_op | source)
XLA Modules:
  0.0 104.1 jit_solution(15032182143192202762)
XLA Ops:
  0.6 1.2 %copy_bitcast_fusion = (bf16[1,2,2,64,128]{4,2,1,0,3:T(2,128)(2,1)S(1)}, bf16[1,2,2,64,128]{4,2,1,0,3:T(2,128)(2,1)S(1)}) fusion(bf16[2,2,64,128]{3,2,1,0:T(8,128)(2,1)} %param.4, bf16[2,2,64,128]{3,2,1,0:T(8,128)(2,1)} %param.5, s32[2,2,64,128]{3,2,1,0:T(8,128)} %param.6), kind=kLoop, calls=%fused_computation.149 | loop fusion | flops 65536 | bytes 393216 | tf_op jit(solution)/shard_map/stack | solution.py:61
  1.8 0.2 pad_maximum_fusion.1
  2.0 27.9 %all_to_all.54 = bf16[2,2,2,64,128]{4,2,1,0,3:T(2,128)(2,1)S(1)} all-to-all(bf16[2,2,2,64,128]{4,2,1,0,3:T(2,128)(2,1)S(1)} %pad_maximum_fusion.1), channel_id=1, replica_groups=mesh['chan'=64,'slab'=4] {'chan'}, dimensions={3} | all-to-all | bytes 262144 | tf_op jit(solution)/shard_map/all_to_all | solution.py:62
  30.1 2.4 %collective-permute-start.1 = (bf16[2,128,2,1,128]{1,4,2,3,0:T(8,128)(2,1)S(1)}, bf16[2,128,2,1,128]{1,4,2,3,0:T(8,128)(2,1)S(1)}, u32[]{:S(2)}, u32[]{:S(2)}) collective-permute-start(bf16[2,128,2,1,128]{1,4,2,3,0:T(8,128)(2,1)S(1)} %copy.21), channel_id=1, source_target_pairs={{4,0},{8,4},{12,8},{16,12},{20,16},{24,20},{28,24},{32,28},{36,32}... | collective-permute-start | bytes 393224 | tf_op jit(solution)/shard_map/ppermute | solution.py:15
  32.6 3.1 %collective-permute-start = (bf16[2,128,2,1,128]{1,4,2,3,0:T(8,128)(2,1)S(1)}, bf16[2,128,2,1,128]{1,4,2,3,0:T(8,128)(2,1)S(1)}, u32[]{:S(2)}, u32[]{:S(2)}) collective-permute-start(bf16[2,128,2,1,128]{1,4,2,3,0:T(8,128)(2,1)S(1)} %copy.21), channel_id=1, source_target_pairs={{0,4},{4,8},{8,12},{12,16},{16,20},{20,24},{24,28},{28,32},{32,36}... | collective-permute-start | bytes 393224 | tf_op jit(solution)/shard_map/ppermute | solution.py:14
  35.7 0.7 collective-permute-done.1
  36.4 1.2 %collective-permute-done = bf16[2,128,2,1,128]{1,4,2,3,0:T(8,128)(2,1)S(1)} collective-permute-done((bf16[2,128,2,1,128]{1,4,2,3,0:T(8,128)(2,1)S(1)}, bf16[2,128,2,1,128]{1,4,2,3,0:T(8,128)(2,1)S(1)}, u32[]{:S(2)}, u32[]{:S(2)}) %collective-permute-start) | collective-permute-done | bytes 131104 | tf_op jit(solution)/shard_map/ppermute | solution.py:14
  37.7 4.0 %collective-permute-start.2 = (bf16[2,128,1,3,128]{1,4,2,3,0:T(8,128)(2,1)S(1)}, bf16[2,128,1,3,128]{1,4,2,3,0:T(8,128)(2,1)S(1)}, u32[]{:S(2)}, u32[]{:S(2)}) collective-permute-start(bf16[2,128,1,3,128]{1,4,2,3,0:T(8,128)(2,1)S(1)} %get-tuple-element.8), channel_id=1, source_target_pairs={{0,1},{1,2},{2,3},{4,5},{5,6},{6,7},{8,9},{9,10},{10,11},{12,13},{... | collective-permute-start | bytes 589832 | tf_op jit(solution)/shard_map/ppermute | solution.py:14
  41.7 1.3 %collective-permute-start.3 = (bf16[2,128,1,3,128]{1,4,2,3,0:T(8,128)(2,1)S(1)}, bf16[2,128,1,3,128]{1,4,2,3,0:T(8,128)(2,1)S(1)}, u32[]{:S(2)}, u32[]{:S(2)}) collective-permute-start(bf16[2,128,1,3,128]{1,4,2,3,0:T(8,128)(2,1)S(1)} %get-tuple-element.9), channel_id=1, source_target_pairs={{1,0},{2,1},{3,2},{5,4},{6,5},{7,6},{9,8},{10,9},{11,10},{13,12},{... | collective-permute-start | bytes 589832 | tf_op jit(solution)/shard_map/ppermute | solution.py:15
  43.0 2.9 %collective-permute-done.2 = bf16[2,128,1,3,128]{1,4,2,3,0:T(8,128)(2,1)S(1)} collective-permute-done((bf16[2,128,1,3,128]{1,4,2,3,0:T(8,128)(2,1)S(1)}, bf16[2,128,1,3,128]{1,4,2,3,0:T(8,128)(2,1)S(1)}, u32[]{:S(2)}, u32[]{:S(2)}) %collective-permute-start.2) | collective-permute-done | bytes 196640 | tf_op jit(solution)/shard_map/ppermute | solution.py:14
  45.9 3.3 %collective-permute-done.3 = bf16[2,128,1,3,128]{1,4,2,3,0:T(8,128)(2,1)S(1)} collective-permute-done((bf16[2,128,1,3,128]{1,4,2,3,0:T(8,128)(2,1)S(1)}, bf16[2,128,1,3,128]{1,4,2,3,0:T(8,128)(2,1)S(1)}, u32[]{:S(2)}, u32[]{:S(2)}) %collective-permute-start.3) | collective-permute-done | bytes 196640 | tf_op jit(solution)/shard_map/ppermute | solution.py:15
  49.2 0.3 select_maximum_fusion
  49.6 1.1 %copy-done = bf16[3,3,3,128,128]{4,3,2,1,0:T(8,128)(2,1)S(1)} copy-done((bf16[3,3,3,128,128]{4,3,2,1,0:T(8,128)(2,1)S(1)}, bf16[3,3,3,128,128]{4,3,2,1,0:T(8,128)(2,1)}, u32[]{:S(2)}) %copy-start) | copy-done | bytes 884760
  50.8 0.1 convolution_bitcast_fusion.1
  52.2 0.2 convolution_bitcast_fusion.10
  52.3 0.2 convolution_bitcast_fusion.11
  52.5 0.2 convolution_bitcast_fusion.12
  52.7 0.2 convolution_bitcast_fusion.13
  52.8 0.2 convolution_bitcast_fusion.14
  53.0 0.2 convolution_bitcast_fusion.15
  53.2 0.2 convolution_bitcast_fusion.16
  53.3 0.2 convolution_bitcast_fusion.17
  53.5 0.2 convolution_bitcast_fusion.18
  53.7 0.2 fusion.33
  53.8 0.2 convolution_add_fusion.15
  54.0 0.1 convolution_add_fusion.14
  54.1 0.1 convolution_add_fusion.13
  54.3 0.2 convolution_add_fusion.12
  54.5 0.2 convolution_add_fusion.11
  54.6 0.1 convolution_add_fusion.10
  54.8 0.2 convolution_add_fusion.9
  54.9 0.2 convolution_add_fusion.8
  55.1 0.1 convolution_add_fusion.7
  55.2 0.2 convolution_add_fusion.6
  55.4 0.2 convolution_add_fusion.5
  55.5 0.1 convolution_add_fusion.4
  56.0 0.2 convolution_add_fusion.1
  56.1 0.2 fusion.21
  56.3 0.2 fusion.26
  56.5 0.8 copy.26
  57.3 17.6 %all-to-all-start.2 = ((bf16[128,2,1,128]{3,1,2,0:T(2,128)(2,1)}), bf16[128,2,1,128]{3,1,2,0:T(2,128)(2,1)S(1)}, u32[]{:S(2)}, u32[]{:S(2)}) async-start(bf16[128,2,1,128]{3,1,2,0:T(2,128)(2,1)} %copy.26), calls=%async_computation.2 | async-start | bytes 131072 | tf_op jit(solution)/shard_map/all_to_all | solution.py:70
  74.9 0.2 convolution_add_fusion.31
  75.0 0.2 convolution_add_fusion.30
  75.2 0.2 convolution_add_fusion.29
  75.4 0.2 convolution_add_fusion.28
  75.5 0.2 convolution_add_fusion.27
  75.7 0.2 convolution_add_fusion.26
  75.9 0.2 convolution_add_fusion.25
  76.1 0.2 convolution_add_fusion.24
  76.2 0.2 convolution_add_fusion.23
  76.4 0.2 convolution_add_fusion.22
  76.6 0.2 convolution_add_fusion.21
  76.7 0.2 convolution_add_fusion.20
  76.9 0.2 convolution_add_fusion.19
  77.1 0.2 convolution_add_fusion.18
  77.3 0.2 convolution_add_fusion.17
  77.4 0.2 fusion.22
  77.6 0.2 fusion.25
  77.8 0.8 copy.24
  78.6 8.3 %all-to-all-done.2 = bf16[128,2,1,128]{3,1,2,0:T(2,128)(2,1)S(1)} async-done(((bf16[128,2,1,128]{3,1,2,0:T(2,128)(2,1)}), bf16[128,2,1,128]{3,1,2,0:T(2,128)(2,1)S(1)}, u32[]{:S(2)}, u32[]{:S(2)}) %all-to-all-start.2) | async-done | bytes 65568 | tf_op jit(solution)/shard_map/all_to_all | solution.py:70
  86.9 4.5 %all-to-all-start.1 = ((bf16[128,2,1,128]{3,1,2,0:T(2,128)(2,1)}), bf16[128,2,1,128]{3,1,2,0:T(2,128)(2,1)S(1)}, u32[]{:S(2)}, u32[]{:S(2)}) async-start(bf16[128,2,1,128]{3,1,2,0:T(2,128)(2,1)} %copy.24), calls=%async_computation.1 | async-start | bytes 131072 | tf_op jit(solution)/shard_map/all_to_all | solution.py:69
  91.4 0.6 copy.29
  92.0 11.4 %all-to-all-done.1 = bf16[128,2,1,128]{3,1,2,0:T(2,128)(2,1)S(1)} async-done(((bf16[128,2,1,128]{3,1,2,0:T(2,128)(2,1)}), bf16[128,2,1,128]{3,1,2,0:T(2,128)(2,1)S(1)}, u32[]{:S(2)}, u32[]{:S(2)}) %all-to-all-start.1) | async-done | bytes 65568 | tf_op jit(solution)/shard_map/all_to_all | solution.py:69
  103.4 0.6 copy.28
  (19 shorter events, 1.9 us)
Async XLA Ops:
  30.1 6.3 %collective-permute-start.1 = (bf16[2,128,2,1,128]{1,4,2,3,0:T(8,128)(2,1)S(1)}, bf16[2,128,2,1,128]{1,4,2,3,0:T(8,128)(2,1)S(1)}, u32[]{:S(2)}, u32[]{:S(2)}) collective-permute-start(bf16[2,128,2,1,128]{1,4,2,3,0:T(8,128)(2,1)S(1)} %copy.21), channel_id=1, source_target_pairs={{4,0},{8,4},{12,8},{16,12},{20,16},{24,20},{28,24},{32,28},{36,32}... | collective-permute-start | bytes 393224 | tf_op jit(solution)/shard_map/ppermute | solution.py:15
  32.6 5.1 %collective-permute-start = (bf16[2,128,2,1,128]{1,4,2,3,0:T(8,128)(2,1)S(1)}, bf16[2,128,2,1,128]{1,4,2,3,0:T(8,128)(2,1)S(1)}, u32[]{:S(2)}, u32[]{:S(2)}) collective-permute-start(bf16[2,128,2,1,128]{1,4,2,3,0:T(8,128)(2,1)S(1)} %copy.21), channel_id=1, source_target_pairs={{0,4},{4,8},{8,12},{12,16},{16,20},{20,24},{24,28},{28,32},{32,36}... | collective-permute-start | bytes 393224 | tf_op jit(solution)/shard_map/ppermute | solution.py:14
  37.7 8.2 %collective-permute-start.2 = (bf16[2,128,1,3,128]{1,4,2,3,0:T(8,128)(2,1)S(1)}, bf16[2,128,1,3,128]{1,4,2,3,0:T(8,128)(2,1)S(1)}, u32[]{:S(2)}, u32[]{:S(2)}) collective-permute-start(bf16[2,128,1,3,128]{1,4,2,3,0:T(8,128)(2,1)S(1)} %get-tuple-element.8), channel_id=1, source_target_pairs={{0,1},{1,2},{2,3},{4,5},{5,6},{6,7},{8,9},{9,10},{10,11},{12,13},{... | collective-permute-start | bytes 589832 | tf_op jit(solution)/shard_map/ppermute | solution.py:14
  41.7 7.5 %collective-permute-start.3 = (bf16[2,128,1,3,128]{1,4,2,3,0:T(8,128)(2,1)S(1)}, bf16[2,128,1,3,128]{1,4,2,3,0:T(8,128)(2,1)S(1)}, u32[]{:S(2)}, u32[]{:S(2)}) collective-permute-start(bf16[2,128,1,3,128]{1,4,2,3,0:T(8,128)(2,1)S(1)} %get-tuple-element.9), channel_id=1, source_target_pairs={{1,0},{2,1},{3,2},{5,4},{6,5},{7,6},{9,8},{10,9},{11,10},{13,12},{... | collective-permute-start | bytes 589832 | tf_op jit(solution)/shard_map/ppermute | solution.py:15
  49.5 1.2 %copy-start = (bf16[3,3,3,128,128]{4,3,2,1,0:T(8,128)(2,1)S(1)}, bf16[3,3,3,128,128]{4,3,2,1,0:T(8,128)(2,1)}, u32[]{:S(2)}) copy-start(bf16[3,3,3,128,128]{4,3,2,1,0:T(8,128)(2,1)} %param.7) | copy-start | bytes 2654212
  57.3 29.6 %all-to-all-start.2 = ((bf16[128,2,1,128]{3,1,2,0:T(2,128)(2,1)}), bf16[128,2,1,128]{3,1,2,0:T(2,128)(2,1)S(1)}, u32[]{:S(2)}, u32[]{:S(2)}) async-start(bf16[128,2,1,128]{3,1,2,0:T(2,128)(2,1)} %copy.26), calls=%async_computation.2 | async-start | bytes 131072 | tf_op jit(solution)/shard_map/all_to_all | solution.py:70
  86.9 16.6 %all-to-all-start.1 = ((bf16[128,2,1,128]{3,1,2,0:T(2,128)(2,1)}), bf16[128,2,1,128]{3,1,2,0:T(2,128)(2,1)S(1)}, u32[]{:S(2)}, u32[]{:S(2)}) async-start(bf16[128,2,1,128]{3,1,2,0:T(2,128)(2,1)} %copy.24), calls=%async_computation.1 | async-start | bytes 131072 | tf_op jit(solution)/shard_map/all_to_all | solution.py:69
where the time goes:
time: 104 us
  starting transfers between devices  32.9 us (32%)
  blocking collectives  27.9 us (27%)
  waiting for transfers between devices  27.8 us (27%)
  matrix products  8.48 us (8%)
  local copies, waits for them, and re-layouts  4.21 us (4%)
  other arithmetic  1.7 us (2%)
  between operations  1.07 us (1%)
    all_to_all x1, blocking collectives, body(): lax.all_to_all(stacked, 'chan', split_axis=3, concat_axis=1, tiled=True)  27.9 us
    all_to_all x1, starting transfers between devices, body(): lax.all_to_all(grad_block, 'chan', split_axis=0, concat_axis=2, tiled=True)  17.6 us
    all_to_all x1, waiting for transfers between devices, body(): lax.all_to_all(pre_block, 'chan', split_axis=0, concat_axis=2, tiled=True)  11.4 us
    all_to_all x1, waiting for transfers between devices, body(): lax.all_to_all(grad_block, 'chan', split_axis=0, concat_axis=2, tiled=True)  8.28 us
    ppermute x2, starting transfers between devices, with_halo(): before = lax.ppermute(last, axis, up)  7.15 us
    all_to_all x1, starting transfers between devices, body(): lax.all_to_all(pre_block, 'chan', split_axis=0, concat_axis=2, tiled=True)  4.48 us
    dot_general x27, matrix products, forward_sum(): jnp.einsum('oi,idhw->odhw', w_rows[i, j, k], windows[tap], preferred_elem...  4.47 us
    ppermute x2, waiting for transfers between devices, with_halo(): before = lax.ppermute(last, axis, up)  4.12 us
  transfers between devices with their start and end apart: 6, of which 6 were waited for; matrix products, arithmetic and copies ran while one was open for 4% of the time, Pallas kernels for 0%

commit v1 on v0

v1 whole, which is shorter than its diff:
```python
import jax
import jax.numpy as jnp
from jax import lax
from jax.experimental import pallas as pl
from jax.experimental.pallas import tpu as pltpu
from jax.sharding import PartitionSpec as P

MESH = pl.DeviceIdType.MESH
BLOCKS = 32
LANES = 128


def spread(height):
    ch = lax.broadcasted_iota(jnp.int32, (3 * LANES, 1), 0)
    tap, ch = lax.shift_right_logical(ch, 7), lax.bitwise_and(ch, 127)
    at = lax.broadcasted_iota(jnp.int32, (1, 4 * LANES), 1)
    z_hi = lax.shift_right_logical(at, 8)
    source = lax.bitwise_and(lax.shift_right_logical(at, 3), 31)
    chan = lax.shift_right_logical(source, 3) * 16 + z_hi * 8 + lax.bitwise_and(source, 7)
    channel = 2 * chan + lax.bitwise_and(lax.shift_right_logical(at, 2), 1)
    hit = (ch == channel) & (lax.bitwise_and(at, 3) == tap + height)
    return jnp.where(hit, 1.0, 0.0).astype(jnp.bfloat16)


def kernel(act, cot, mask, weights, landed, act_v, cot_v, mask_v, w_v, padded, send, recv, taps, rows_f, units_f, out_send,
           in_sem, w_sem, send_sem, adj_sem, recv_sem, out_send_sem, out_recv_sem):
    chan, slab = lax.axis_index("chan"), lax.axis_index("slab")
    z_hi = (chan // 8) % 2
    core = chan % 2
    source = (chan // 16) * 8 + chan % 8
    worker = z_hi == 0
    pair = slab // 2
    work_pair = 1 - slab // 2
    work_adj = 2 - work_pair
    adj = (slab == 1) | (slab == 2)
    my_block = ((chan // 16) * 4 + (chan // 2) % 4) * 2 + slab % 2

    loads = [
        pltpu.make_async_copy(act, act_v, in_sem.at[0]),
        pltpu.make_async_copy(cot, cot_v, in_sem.at[1]),
        pltpu.make_async_copy(mask, mask_v, in_sem.at[2]),
    ]
    for load in loads:
        load.start()
    w_load = pltpu.make_async_copy(weights, w_v, w_sem)

    barrier = pltpu.get_barrier_semaphore()

    @pl.when(worker)
    def _():
        @pl.loop(0, 64)
        def _(other):
            for q in range(2):
                pl.semaphore_signal(barrier, inc=1, device_id=(other, 2 * work_pair + q), device_id_type=MESH)

            @pl.when((other != chan) | (work_adj != slab))
            def _():
                pl.semaphore_signal(barrier, inc=1, device_id=(other, work_adj), device_id_type=MESH)

        w_load.start()

    for load in loads:
        load.wait()
    for c in range(2):
        for ch in range(2):
            for p in range(2):
                padded[c, ch, p, 0:8, :] = jnp.zeros((8, LANES), jnp.float32)
                padded[c, ch, p, 72:80, :] = jnp.zeros((8, LANES), jnp.float32)
    for ch in range(2):
        for p in range(2):
            padded[0, ch, p, 8:72, :] = act_v[ch, p].astype(jnp.float32)
            padded[1, ch, p, 8:72, :] = jnp.where(mask_v[ch, p] == 1, cot_v[ch, p].astype(jnp.float32), 0.0)
    for b in range(BLOCKS):
        for c in range(2):
            for p in range(2):
                window = [padded[c, ch, p, 7 + 2 * b : 11 + 2 * b, :] for ch in range(2)]
                send[2 * b + c, p] = jnp.concatenate(window, axis=0).astype(jnp.bfloat16)

    itself = worker & adj
    pl.semaphore_wait(barrier, 64 + 64 * adj.astype(jnp.int32) - itself.astype(jnp.int32))

    def target(step, c, zb, of_pair):
        at = (step + chan // 2) % 16
        other = (at // 4) * 16 + (at % 4) * 2 + c
        return (other, 2 * (1 - of_pair) + zb), (at * 2 + zb) * 2 + c

    @pl.loop(0, 16)
    def _(step):
        for zb in range(2):
            for c in range(2):
                device, unit = target(step, c, zb, pair)
                pltpu.make_async_remote_copy(
                    src_ref=send.at[unit],
                    dst_ref=recv.at[z_hi, pl.ds(1 + 2 * (slab % 2), 2), source],
                    send_sem=send_sem,
                    recv_sem=recv_sem.at[z_hi],
                    device_id=device,
                    device_id_type=MESH,
                ).start()

    @pl.when(adj)
    def _():
        plane = 2 - slab
        there = 5 * (slab - 1)

        @pl.loop(0, 16)
        def _(step):
            for zb in range(2):
                for c in range(2):
                    (other, at_slab), unit = target(step, c, zb, 1 - pair)
                    remote = (other != chan) | (at_slab != slab)

                    @pl.when(remote)
                    def _():
                        pltpu.make_async_remote_copy(
                            src_ref=send.at[unit, plane],
                            dst_ref=recv.at[z_hi, there, source],
                            send_sem=adj_sem,
                            recv_sem=recv_sem.at[z_hi],
                            device_id=(other, at_slab),
                            device_id_type=MESH,
                        ).start()

                    @pl.when(jnp.logical_not(remote))
                    def _():
                        pltpu.make_async_copy(send.at[unit, plane], recv.at[z_hi, there, source], recv_sem.at[z_hi]).start()

    @pl.when(worker)
    def _():
        recv[:, 5 * work_pair] = jnp.zeros((2, 32, 8, LANES), jnp.bfloat16)
        w_load.wait()
        for height in range(2):
            places = spread(height)
            for i in range(3):

                @pl.loop(0, 3)
                def _(k):
                    at = pl.ds(pl.multiple_of(k * LANES, LANES), LANES)

                    @pl.when(core == 0)
                    def _():
                        left = jnp.concatenate([w_v[i, j, k] for j in range(3)], axis=1)
                        total = jnp.dot(left, places, preferred_element_type=jnp.float32)
                        taps[height, at, 512 * i : 512 * (i + 1)] = total.astype(jnp.bfloat16)

                    @pl.when(core == 1)
                    def _():
                        left = jnp.concatenate([w_v[2 - i, 2 - j, 2 - k] for j in range(3)], axis=0)
                        total = lax.dot_general(
                            left, places, (((0,), (0,)), ((), ())), preferred_element_type=jnp.float32
                        )
                        taps[height, at, 512 * i : 512 * (i + 1)] = total.astype(jnp.bfloat16)

        for half in range(2):
            here = recv.at[half, pl.ds(1 - work_pair, 5)]
            pltpu.make_async_copy(here, here, recv_sem.at[half]).wait()

        col = lax.broadcasted_iota(jnp.int32, (LANES, LANES), 1)
        for q in range(2):
            held = [
                [recv[half, 2 * q + i].reshape(256, LANES) for half in range(2)] for i in range(4)
            ]
            right = jnp.concatenate(
                [jnp.concatenate([held[i][half], held[i + 1][half]], axis=1) for i in range(3) for half in range(2)], axis=0
            )
            for height in range(2):
                part = jnp.dot(taps[height], right, preferred_element_type=jnp.float32)
                for p in range(2):
                    lanes = slice(LANES * p, LANES * (p + 1))
                    before, here, after = (part[LANES * k : LANES * (k + 1), lanes] for k in range(3))
                    total = (
                        here
                        + jnp.where(col == 0, 0.0, pltpu.roll(before, 1, 1))
                        + jnp.where(col == LANES - 1, 0.0, pltpu.roll(after, LANES - 1, 1))
                    )
                    rows_f[p, height] = total
            for p in range(2):
                for height in range(2):
                    for ch in range(2):
                        units_f[pl.ds(4 * p + 2 * height + ch, 64, stride=8), :] = rows_f[
                            p, height, pl.ds(ch, 64, stride=2), :
                        ]
            out_send[q] = units_f[...].astype(jnp.bfloat16).reshape(64, 8, LANES)

        for half in range(2):

            @pl.loop(0, 32)
            def _(step):
                other = (step // 8) * 16 + half * 8 + step % 8
                for q in range(2):
                    pltpu.make_async_remote_copy(
                        src_ref=out_send.at[q, other],
                        dst_ref=landed.at[core, my_block],
                        send_sem=out_send_sem,
                        recv_sem=out_recv_sem,
                        device_id=(other, 2 * work_pair + q),
                        device_id_type=MESH,
                    ).start()

    pltpu.make_async_copy(landed, landed, out_recv_sem).wait()

    pltpu.make_async_copy(send, send, send_sem).wait()

    @pl.when(adj & jnp.logical_not(worker))
    def _():
        half = send.at[pl.ds(0, 32)]
        pltpu.make_async_copy(half, half, adj_sem).wait()

    @pl.when(itself)
    def _():
        short = send.at[pl.ds(0, 63), 0]
        pltpu.make_async_copy(short, short, adj_sem).wait()

    @pl.when(worker)
    def _():
        pltpu.make_async_copy(out_send, out_send, out_send_sem).wait()


def order_rows(landed, pre, grad, landed_f, rows_f):
    for c, out in enumerate((pre, grad)):
        landed_f[...] = landed[c].reshape(BLOCKS * 8, LANES).astype(jnp.float32)
        for ch in range(2):
            for p in range(2):
                for height in range(2):
                    rows_f[pl.ds(height, BLOCKS, stride=2), :] = landed_f[
                        pl.ds(4 * p + 2 * height + ch, BLOCKS, stride=8), :
                    ]
                out[ch, p] = rows_f[...].astype(jnp.bfloat16)


def body(activations, cotangent, relu_mask, weights):
    bf16, f32 = jnp.bfloat16, jnp.float32
    vmem, anywhere = pl.BlockSpec(memory_space=pltpu.VMEM), pl.BlockSpec(memory_space=pl.ANY)
    dma = pltpu.SemaphoreType.DMA
    landed = pl.pallas_call(
        kernel,
        out_shape=jax.ShapeDtypeStruct((2, BLOCKS, 8, LANES), bf16),
        in_specs=[anywhere] * 4,
        out_specs=vmem,
        scratch_shapes=[
            pltpu.VMEM((2, 2, 64, LANES), bf16),
            pltpu.VMEM((2, 2, 64, LANES), bf16),
            pltpu.VMEM((2, 2, 64, LANES), jnp.int32),
            pltpu.VMEM((3, 3, 3, LANES, LANES), bf16),
            pltpu.VMEM((2, 2, 2, 80, LANES), f32),
            pltpu.VMEM((2 * BLOCKS, 2, 8, LANES), bf16),
            pltpu.VMEM((2, 6, 32, 8, LANES), bf16),
            pltpu.VMEM((2, 3 * LANES, 12 * LANES), bf16),
            pltpu.VMEM((2, 2, LANES, LANES), f32),
            pltpu.VMEM((64 * 8, LANES), f32),
            pltpu.VMEM((2, 64, 8, LANES), bf16),
            dma((3,)),
            dma,
            dma,
            dma,
            dma((2,)),
            dma,
            dma,
        ],
        compiler_params=pltpu.CompilerParams(
            collective_id=0, has_side_effects=True, vmem_limit_bytes=48 * 1024 * 1024
        ),
    )(activations, cotangent, relu_mask, weights)
    out = jax.ShapeDtypeStruct((2, 2, 64, LANES), bf16)
    return pl.pallas_call(
        order_rows,
        out_shape=(out, out),
        in_specs=[vmem],
        out_specs=(vmem, vmem),
        scratch_shapes=[pltpu.VMEM((BLOCKS * 8, LANES), f32), pltpu.VMEM((64, LANES), f32)],
    )(landed)


def solution(mesh):
    placed = (
        P("chan", "slab", None, None),
        P("chan", "slab", None, None),
        P("chan", "slab", None, None),
        P(),
    )
    return jax.shard_map(
        body,
        mesh=mesh,
        in_specs=placed,
        out_specs=(P("chan", "slab", None, None), P("chan", "slab", None, None)),
        check_vma=False,
    )
```

time: 104 us -> 47.5 us (0.46)
  Pallas kernels: 0 us -> 42.2 us
  starting transfers between devices: 32.9 us -> 0 us
  blocking collectives: 27.9 us -> 0 us
  waiting for transfers between devices: 27.8 us -> 0 us
  matrix products: 8.48 us -> 0 us
  other arithmetic: 1.7 us -> 0 us
    pallas_call x0 -> x2, Pallas kernels: none -> 42.2 us  [the longest x1 40.5 us: body(): pl.pallas_call(kernel, out_shape=jax.ShapeDtypeStruct((2, BLOCKS, 8, LANE...]
    all_to_all x1 -> x0, blocking collectives: 27.9 us -> none  [body(): lax.all_to_all(stacked, 'chan', split_axis=3, concat_axis=1, tiled=True)]
    all_to_all x2 -> x0, starting transfers between devices: 22.1 us -> none  [the longest x1 17.6 us: body(): lax.all_to_all(grad_block, 'chan', split_axis=0, concat_axis=2, tiled=True)]
    all_to_all x2 -> x0, waiting for transfers between devices: 19.7 us -> none  [the longest x1 11.4 us: body(): lax.all_to_all(pre_block, 'chan', split_axis=0, concat_axis=2, tiled=True)]
    ppermute x4 -> x0, starting transfers between devices: 10.9 us -> none  [the longest x2 7.15 us: with_halo(): before = lax.ppermute(last, axis, up)]
    dot_general x54 -> x0, matrix products: 8.48 us -> none  [the longest x27 4.47 us: forward_sum(): jnp.einsum('oi,idhw->odhw', w_rows[i, j, k], windows[tap], preferred_elem...]
    ppermute x4 -> x0, waiting for transfers between devices: 8.08 us -> none  [the longest x2 4.12 us: with_halo(): before = lax.ppermute(last, axis, up)]
    unnamed x4 -> x10, local copies, waits for them, and re-layouts: 2.37 us -> 4.39 us
  transfers between devices with their start and end apart: 6 -> 0, of which waited for: 6 -> 0; matrix products, arithmetic and copies ran while one was open for 4% -> 0% of each run, Pallas kernels for 0% -> 0%
where the time goes in v1:
time: 47.5 us; the launch traced here: 47.2 us
  Pallas kernels  42.2 us (89%)
  local copies, waits for them, and re-layouts  4.39 us (9%)
  between operations  0.66 us (1%)
    pallas_call x1, Pallas kernels, body(): pl.pallas_call(kernel, out_shape=jax.ShapeDtypeStruct((2, BLOCKS, 8, LANE...  40.5 us
    unnamed x10, local copies, waits for them, and re-layouts  4.39 us
    pallas_call x1, Pallas kernels, body(): pl.pallas_call(order_rows, out_shape=(out, out), in_specs=[vmem], out_spe...  1.63 us

profile of v1, /device:TPU:1, one launch (start us, length us, event | category | flops | bytes accessed | tf_op | source)
XLA Modules:
  0.0 47.2 jit_solution(6231256799521099213)
XLA Ops:
  0.6 0.0 copy-start
  0.6 1.2 %copy-done = bf16[3,3,3,128,128]{4,3,2,1,0:T(8,128)(2,1)S(1)} copy-done((bf16[3,3,3,128,128]{4,3,2,1,0:T(8,128)(2,1)S(1)}, bf16[3,3,3,128,128]{4,3,2,1,0:T(8,128)(2,1)}, u32[]{:S(2)}) %copy-start) | copy-done | bytes 884760
  1.8 0.0 copy-start.2
  1.8 0.9 %copy-done.2 = s32[2,2,64,128]{3,2,1,0:T(8,128)S(1)} copy-done((s32[2,2,64,128]{3,2,1,0:T(8,128)S(1)}, s32[2,2,64,128]{3,2,1,0:T(8,128)}, u32[]{:S(2)}) %copy-start.2) | copy-done | bytes 131096
  2.7 0.0 copy-start.3
  2.7 0.8 %copy-done.3 = bf16[2,2,64,128]{3,2,1,0:T(8,128)(2,1)S(1)} copy-done((bf16[2,2,64,128]{3,2,1,0:T(8,128)(2,1)S(1)}, bf16[2,2,64,128]{3,2,1,0:T(8,128)(2,1)}, u32[]{:S(2)}) %copy-start.3) | copy-done | bytes 65560
  3.5 0.0 copy-start.4
  3.5 0.8 %copy-done.4 = bf16[2,2,64,128]{3,2,1,0:T(8,128)(2,1)S(1)} copy-done((bf16[2,2,64,128]{3,2,1,0:T(8,128)(2,1)S(1)}, bf16[2,2,64,128]{3,2,1,0:T(8,128)(2,1)}, u32[]{:S(2)}) %copy-start.4) | copy-done | bytes 65560
  4.4 40.5 %shard_map.59.landed = bf16[2,32,8,128]{3,2,1,0:T(8,128)(2,1)S(1)} custom-call(bf16[2,2,64,128]{3,2,1,0:T(8,128)(2,1)S(1)} %copy-done.3, bf16[2,2,64,128]{3,2,1,0:T(8,128)(2,1)S(1)} %copy-done.4, s32[2,2,64,128]{3,2,1,0:T(8,128)S(1)} %copy-done.2, bf16[3,3,3,128,128]{4,3,2,1,0:T(8,128)(2,1)S(1)} %copy-done), custom_call_target="tpu_custom_call" | custom-call | tf_op jit(solution)/shard_map/pallas_call | solution.py:235
  44.9 0.0 copy-start.1
  44.9 0.6 %copy-done.1 = bf16[2,32,8,128]{3,2,1,0:T(8,128)(2,1)} copy-done((bf16[2,32,8,128]{3,2,1,0:T(8,128)(2,1)}, bf16[2,32,8,128]{3,2,1,0:T(8,128)(2,1)S(1)}, u32[]{:S(2)}) %copy-start.1) | copy-done | bytes 131096
  45.6 1.6 %shard_map.60 = (bf16[2,2,64,128]{3,2,1,0:T(8,128)(2,1)}, bf16[2,2,64,128]{3,2,1,0:T(8,128)(2,1)}) custom-call(bf16[2,32,8,128]{3,2,1,0:T(8,128)(2,1)} %copy-done.1), custom_call_target="tpu_custom_call" | custom-call | tf_op jit(solution)/shard_map/pallas_call | solution.py:265
Async XLA Ops:
  0.6 1.2 %copy-start = (bf16[3,3,3,128,128]{4,3,2,1,0:T(8,128)(2,1)S(1)}, bf16[3,3,3,128,128]{4,3,2,1,0:T(8,128)(2,1)}, u32[]{:S(2)}) copy-start(bf16[3,3,3,128,128]{4,3,2,1,0:T(8,128)(2,1)} %weights.1) | copy-start | bytes 2654212
  1.8 0.9 %copy-start.2 = (s32[2,2,64,128]{3,2,1,0:T(8,128)S(1)}, s32[2,2,64,128]{3,2,1,0:T(8,128)}, u32[]{:S(2)}) copy-start(s32[2,2,64,128]{3,2,1,0:T(8,128)} %mask.1) | copy-start | bytes 393220
  2.7 0.8 %copy-start.3 = (bf16[2,2,64,128]{3,2,1,0:T(8,128)(2,1)S(1)}, bf16[2,2,64,128]{3,2,1,0:T(8,128)(2,1)}, u32[]{:S(2)}) copy-start(bf16[2,2,64,128]{3,2,1,0:T(8,128)(2,1)} %act.1) | copy-start | bytes 196612
  3.5 0.8 %copy-start.4 = (bf16[2,2,64,128]{3,2,1,0:T(8,128)(2,1)S(1)}, bf16[2,2,64,128]{3,2,1,0:T(8,128)(2,1)}, u32[]{:S(2)}) copy-start(bf16[2,2,64,128]{3,2,1,0:T(8,128)(2,1)} %cot.1) | copy-start | bytes 196612
  44.9 0.7 %copy-start.1 = (bf16[2,32,8,128]{3,2,1,0:T(8,128)(2,1)}, bf16[2,32,8,128]{3,2,1,0:T(8,128)(2,1)S(1)}, u32[]{:S(2)}) copy-start(bf16[2,32,8,128]{3,2,1,0:T(8,128)(2,1)S(1)} %shard_map.59.landed) | copy-start | bytes 393220

commit v2 on v1

v2 whole, which is shorter than its diff:
```python
import jax
import jax.numpy as jnp
from jax import lax
from jax.experimental import pallas as pl
from jax.experimental.pallas import tpu as pltpu
from jax.sharding import PartitionSpec as P

MESH = pl.DeviceIdType.MESH
BLOCKS = 32
LANES = 128


def spread(height):
    ch = lax.broadcasted_iota(jnp.int32, (3 * LANES, 1), 0)
    tap, ch = lax.shift_right_logical(ch, 7), lax.bitwise_and(ch, 127)
    at = lax.broadcasted_iota(jnp.int32, (1, 4 * LANES), 1)
    z_hi = lax.shift_right_logical(at, 8)
    source = lax.bitwise_and(lax.shift_right_logical(at, 3), 31)
    chan = lax.shift_right_logical(source, 3) * 16 + z_hi * 8 + lax.bitwise_and(source, 7)
    channel = 2 * chan + lax.bitwise_and(lax.shift_right_logical(at, 2), 1)
    hit = (ch == channel) & (lax.bitwise_and(at, 3) == tap + height)
    return jnp.where(hit, 1.0, 0.0).astype(jnp.bfloat16)


def kernel(act, cot, mask, weights, landed, act_v, cot_v, mask_v, w_v, padded, send, recv, taps, part_f, rows_f, units_f,
           out_send, in_sem, w_sem, send_sem, adj_sem, recv_sem, side_send_sem, side_recv_sem, out_send_sem,
           out_recv_sem):
    chan, slab = lax.axis_index("chan"), lax.axis_index("slab")
    z_hi = (chan // 8) % 2
    core = chan % 2
    beside = chan + 1 - 2 * core
    source = (chan // 16) * 8 + chan % 8
    pair = slab // 2
    adj = (slab == 1) | (slab == 2)
    my_block = ((chan // 16) * 4 + (chan // 2) % 4) * 2 + slab % 2
    work = 2 * (1 - slab // 2) + core
    work_inner = (work == 1) | (work == 2)
    work_adj = 3 - work
    itself = adj & (core == slab - 1)

    loads = [
        pltpu.make_async_copy(act, act_v, in_sem.at[0]),
        pltpu.make_async_copy(cot, cot_v, in_sem.at[1]),
        pltpu.make_async_copy(mask, mask_v, in_sem.at[2]),
    ]
    for load in loads:
        load.start()
    w_load = pltpu.make_async_copy(weights, w_v, w_sem)
    w_load.start()

    barrier = pltpu.get_barrier_semaphore()
    pl.semaphore_signal(barrier, inc=1, device_id=(beside, slab), device_id_type=MESH)
    for other in range(64):
        pl.semaphore_signal(barrier, inc=1, device_id=(other, work), device_id_type=MESH)

    @pl.when(work_inner)
    def _():
        @pl.loop(0, 64)
        def _(other):
            @pl.when((other != chan) | (work_adj != slab))
            def _():
                pl.semaphore_signal(barrier, inc=1, device_id=(other, work_adj), device_id_type=MESH)

    for load in loads:
        load.wait()
    for c in range(2):
        for ch in range(2):
            for p in range(2):
                padded[c, ch, p, 0:8, :] = jnp.zeros((8, LANES), jnp.float32)
                padded[c, ch, p, 72:80, :] = jnp.zeros((8, LANES), jnp.float32)
    for ch in range(2):
        for p in range(2):
            padded[0, ch, p, 8:72, :] = act_v[ch, p].astype(jnp.float32)
            padded[1, ch, p, 8:72, :] = jnp.where(mask_v[ch, p] == 1, cot_v[ch, p].astype(jnp.float32), 0.0)
    for b in range(BLOCKS):
        for c in range(2):
            for p in range(2):
                window = [padded[c, ch, p, 7 + 2 * b : 11 + 2 * b, :] for ch in range(2)]
                send[2 * b + c, p] = jnp.concatenate(window, axis=0).astype(jnp.bfloat16)

    pl.semaphore_wait(barrier, 65 + 64 * adj.astype(jnp.int32) - itself.astype(jnp.int32))

    for c in (1, 0):
        for b in range(BLOCKS):
            pltpu.make_async_remote_copy(
                src_ref=send.at[2 * b + c],
                dst_ref=recv.at[z_hi, pl.ds(1, 2), source],
                send_sem=send_sem,
                recv_sem=recv_sem.at[z_hi],
                device_id=((b // 8) * 16 + 8 * c + (b // 2 % 4) * 2 + slab % 2, 2 * (1 - pair) + b % 2),
                device_id_type=MESH,
            ).start()

    @pl.when(adj)
    def _():
        plane = 2 - slab
        there = 3 * (slab - 1)
        for c in (1, 0):

            @pl.loop(0, BLOCKS)
            def _(b):
                other, at_slab = (b // 8) * 16 + 8 * c + (b // 2 % 4) * 2 + slab - 1, 2 * pair + b % 2
                remote = (other != chan) | (at_slab != slab)

                @pl.when(remote)
                def _():
                    pltpu.make_async_remote_copy(
                        src_ref=send.at[2 * b + c, plane],
                        dst_ref=recv.at[z_hi, there, source],
                        send_sem=adj_sem,
                        recv_sem=recv_sem.at[z_hi],
                        device_id=(other, at_slab),
                        device_id_type=MESH,
                    ).start()

                @pl.when(jnp.logical_not(remote))
                def _():
                    pltpu.make_async_copy(send.at[2 * b + c, plane], recv.at[z_hi, there, source], recv_sem.at[z_hi]).start()

    @pl.when(jnp.logical_not(work_inner))
    def _():
        recv[:, work] = jnp.zeros((2, 32, 8, LANES), jnp.bfloat16)

    w_load.wait()
    for height in range(2):
        places = spread(height)
        for i in range(3):

            @pl.loop(0, 3)
            def _(k):
                at = pl.ds(pl.multiple_of(k * LANES, LANES), LANES)

                @pl.when(z_hi == 0)
                def _():
                    left = jnp.concatenate([w_v[i, j, k] for j in range(3)], axis=1)
                    total = jnp.dot(left, places, preferred_element_type=jnp.float32)
                    taps[i, height, at, :] = total.astype(jnp.bfloat16)

                @pl.when(z_hi == 1)
                def _():
                    left = jnp.concatenate([w_v[2 - i, 2 - j, 2 - k] for j in range(3)], axis=0)
                    total = lax.dot_general(
                        left, places, (((0,), (0,)), ((), ())), preferred_element_type=jnp.float32
                    )
                    taps[i, height, at, :] = total.astype(jnp.bfloat16)

    for half in range(2):

        @pl.when(work_inner)
        def _():
            here = recv.at[half, pl.ds(2 - work, 3)]
            pltpu.make_async_copy(here, here, recv_sem.at[half]).wait()

        @pl.when(jnp.logical_not(work_inner))
        def _():
            here = recv.at[half, pl.ds(1, 2)]
            pltpu.make_async_copy(here, here, recv_sem.at[half]).wait()

    side = pltpu.make_async_remote_copy(
        src_ref=recv.at[:, 2 - core],
        dst_ref=recv.at[:, 3 * core],
        send_sem=side_send_sem,
        recv_sem=side_recv_sem,
        device_id=(beside, slab),
        device_id_type=MESH,
    )
    side.start()

    def right(i):
        held = [[recv[half, i + p].reshape(256, LANES) for p in range(2)] for half in range(2)]
        return jnp.concatenate([jnp.concatenate(planes, axis=1) for planes in held], axis=0)

    last = 2 - 2 * core
    for height in range(2):
        part_f[height] = jnp.dot(
            taps[1, height], right(1), preferred_element_type=jnp.float32
        ) + jnp.dot(taps[2 - last, height], right(2 - last), preferred_element_type=jnp.float32)
    side.wait_recv()
    col = lax.broadcasted_iota(jnp.int32, (LANES, LANES), 1)
    for height in range(2):
        part = part_f[height] + jnp.dot(taps[last, height], right(last), preferred_element_type=jnp.float32)
        for p in range(2):
            lanes = slice(LANES * p, LANES * (p + 1))
            before, here, after = (part[LANES * k : LANES * (k + 1), lanes] for k in range(3))
            rows_f[p, height] = (
                here
                + jnp.where(col == 0, 0.0, pltpu.roll(before, 1, 1))
                + jnp.where(col == LANES - 1, 0.0, pltpu.roll(after, LANES - 1, 1))
            )
    for p in range(2):
        for height in range(2):
            for ch in range(2):
                units_f[pl.ds(4 * p + 2 * height + ch, 64, stride=8), :] = rows_f[p, height, pl.ds(ch, 64, stride=2), :]
    out_send[...] = units_f[...].astype(jnp.bfloat16).reshape(64, 8, LANES)

    for half in range(2):
        for step in range(32):
            other = (step // 8) * 16 + half * 8 + step % 8
            pltpu.make_async_remote_copy(
                src_ref=out_send.at[other],
                dst_ref=landed.at[z_hi, my_block],
                send_sem=out_send_sem,
                recv_sem=out_recv_sem,
                device_id=(other, work),
                device_id_type=MESH,
            ).start()

    pltpu.make_async_copy(landed, landed, out_recv_sem).wait()
    side.wait_send()
    pltpu.make_async_copy(send, send, send_sem).wait()

    @pl.when(adj & jnp.logical_not(itself))
    def _():
        sent = send.at[:, 0]
        pltpu.make_async_copy(sent, sent, adj_sem).wait()

    @pl.when(itself)
    def _():
        sent = send.at[pl.ds(0, 63), 0]
        pltpu.make_async_copy(sent, sent, adj_sem).wait()

    pltpu.make_async_copy(out_send, out_send, out_send_sem).wait()


def order_rows(landed, pre, grad, landed_f, rows_f):
    for c, out in enumerate((pre, grad)):
        landed_f[...] = landed[c].reshape(BLOCKS * 8, LANES).astype(jnp.float32)
        for ch in range(2):
            for p in range(2):
                for height in range(2):
                    rows_f[pl.ds(height, BLOCKS, stride=2), :] = landed_f[
                        pl.ds(4 * p + 2 * height + ch, BLOCKS, stride=8), :
                    ]
                out[ch, p] = rows_f[...].astype(jnp.bfloat16)


def body(activations, cotangent, relu_mask, weights):
    bf16, f32 = jnp.bfloat16, jnp.float32
    vmem, anywhere = pl.BlockSpec(memory_space=pltpu.VMEM), pl.BlockSpec(memory_space=pl.ANY)
    dma = pltpu.SemaphoreType.DMA
    landed = pl.pallas_call(
        kernel,
        out_shape=jax.ShapeDtypeStruct((2, BLOCKS, 8, LANES), bf16),
        in_specs=[anywhere] * 4,
        out_specs=vmem,
        scratch_shapes=[
            pltpu.VMEM((2, 2, 64, LANES), bf16),
            pltpu.VMEM((2, 2, 64, LANES), bf16),
            pltpu.VMEM((2, 2, 64, LANES), jnp.int32),
            pltpu.VMEM((3, 3, 3, LANES, LANES), bf16),
            pltpu.VMEM((2, 2, 2, 80, LANES), f32),
            pltpu.VMEM((2 * BLOCKS, 2, 8, LANES), bf16),
            pltpu.VMEM((2, 4, 32, 8, LANES), bf16),
            pltpu.VMEM((3, 2, 3 * LANES, 4 * LANES), bf16),
            pltpu.VMEM((2, 3 * LANES, 2 * LANES), f32),
            pltpu.VMEM((2, 2, LANES, LANES), f32),
            pltpu.VMEM((64 * 8, LANES), f32),
            pltpu.VMEM((64, 8, LANES), bf16),
            dma((3,)),
            dma,
            dma,
            dma,
            dma((2,)),
            dma,
            dma,
            dma,
            dma,
        ],
        compiler_params=pltpu.CompilerParams(
            collective_id=0, has_side_effects=True, vmem_limit_bytes=63 * 1024 * 1024
        ),
    )(activations, cotangent, relu_mask, weights)
    out = jax.ShapeDtypeStruct((2, 2, 64, LANES), bf16)
    return pl.pallas_call(
        order_rows,
        out_shape=(out, out),
        in_specs=[vmem],
        out_specs=(vmem, vmem),
        scratch_shapes=[pltpu.VMEM((BLOCKS * 8, LANES), f32), pltpu.VMEM((64, LANES), f32)],
    )(landed)


def solution(mesh):
    placed = (
        P("chan", "slab", None, None),
        P("chan", "slab", None, None),
        P("chan", "slab", None, None),
        P(),
    )
    return jax.shard_map(
        body,
        mesh=mesh,
        in_specs=placed,
        out_specs=(P("chan", "slab", None, None), P("chan", "slab", None, None)),
        check_vma=False,
    )
```

time: 47.5 us -> 37.4 us (0.79)
  Pallas kernels: 42.2 us -> 36.7 us
  local copies, waits for them, and re-layouts: 4.39 us -> 0 us
    pallas_call x1, Pallas kernels: 40.5 us -> 35.1 us  [body(): pl.pallas_call(kernel, out_shape=jax.ShapeDtypeStruct((2, BLOCKS, 8, LANE...]
    unnamed x10 -> x0, local copies, waits for them, and re-layouts: 4.39 us -> none
where the time goes in v2:
time: 37.4 us; the launch traced here: 37.3 us
  Pallas kernels  36.7 us (98%)
  between operations  0.64 us (2%)
    pallas_call x1, Pallas kernels, body(): pl.pallas_call(kernel, out_shape=jax.ShapeDtypeStruct((2, BLOCKS, 8, LANE...  35.1 us
    pallas_call x1, Pallas kernels, body(): pl.pallas_call(order_rows, out_shape=(out, out), in_specs=[vmem], out_spe...  1.63 us

profile of v2, /device:TPU:1, one launch (start us, length us, event | category | flops | bytes accessed | tf_op | source)
XLA Modules:
  0.0 37.3 jit_solution(13434876614598731767)
XLA Ops:
  0.6 35.1 %shard_map.59.landed = bf16[2,32,8,128]{3,2,1,0:T(8,128)(2,1)} custom-call(bf16[2,2,64,128]{3,2,1,0:T(8,128)(2,1)} %act.1, bf16[2,2,64,128]{3,2,1,0:T(8,128)(2,1)} %cot.1, s32[2,2,64,128]{3,2,1,0:T(8,128)} %mask.1, bf16[3,3,3,128,128]{4,3,2,1,0:T(8,128)(2,1)} %weights.1), custom_call_target="tpu_custom_call" | custom-call | tf_op jit(solution)/shard_map/pallas_call | solution.py:241
  35.7 1.6 %shard_map.60 = (bf16[2,2,64,128]{3,2,1,0:T(8,128)(2,1)}, bf16[2,2,64,128]{3,2,1,0:T(8,128)(2,1)}) custom-call(bf16[2,32,8,128]{3,2,1,0:T(8,128)(2,1)} %shard_map.59.landed), custom_call_target="tpu_custom_call" | custom-call | tf_op jit(solution)/shard_map/pallas_call | solution.py:274

commit v3 on v2

--- a/solution.py
+++ b/solution.py
@@ -23,7 +23,7 @@
 
 
 def kernel(act, cot, mask, weights, landed, act_v, cot_v, mask_v, w_v, padded, send, recv, taps, part_f, rows_f, units_f,
-           out_send, in_sem, w_sem, send_sem, adj_sem, recv_sem, side_send_sem, side_recv_sem, out_send_sem,
+           out_send, in_sem, w_sem, send_sem, adj_sem, recv_sem, adj_recv_sem, side_send_sem, side_recv_sem, out_send_sem,
            out_recv_sem):
     chan, slab = lax.axis_index("chan"), lax.axis_index("slab")
     z_hi = (chan // 8) % 2
@@ -78,6 +78,30 @@
                 window = [padded[c, ch, p, 7 + 2 * b : 11 + 2 * b, :] for ch in range(2)]
                 send[2 * b + c, p] = jnp.concatenate(window, axis=0).astype(jnp.bfloat16)
 
+    def make_taps(transposed):
+        w_load.wait()
+        for height in range(2):
+            places = spread(height)
+            for i in range(3):
+
+                @pl.loop(0, 3)
+                def _(k):
+                    if transposed:
+                        left = jnp.concatenate([w_v[2 - i, 2 - j, 2 - k] for j in range(3)], axis=0)
+                        total = lax.dot_general(
+                            left, places, (((0,), (0,)), ((), ())), preferred_element_type=jnp.float32
+                        )
+                    else:
+                        left = jnp.concatenate([w_v[i, j, k] for j in range(3)], axis=1)
+                        total = jnp.dot(left, places, preferred_element_type=jnp.float32)
+                    at = pl.ds(pl.multiple_of(k * LANES, LANES), LANES)
+                    for half in range(2):
+                        taps[i, height, half, at, :] = total[:, 256 * half : 256 * (half + 1)].astype(jnp.bfloat16)
+
+    @pl.when(z_hi == 0)
+    def _():
+        make_taps(False)
+
     pl.semaphore_wait(barrier, 65 + 64 * adj.astype(jnp.int32) - itself.astype(jnp.int32))
 
     for c in (1, 0):
@@ -96,89 +120,74 @@
         plane = 2 - slab
         there = 3 * (slab - 1)
         for c in (1, 0):
-
-            @pl.loop(0, BLOCKS)
-            def _(b):
+            for b in range(BLOCKS):
                 other, at_slab = (b // 8) * 16 + 8 * c + (b // 2 % 4) * 2 + slab - 1, 2 * pair + b % 2
-                remote = (other != chan) | (at_slab != slab)
-
-                @pl.when(remote)
+
+                @pl.when((other != chan) | (at_slab != slab))
                 def _():
                     pltpu.make_async_remote_copy(
                         src_ref=send.at[2 * b + c, plane],
                         dst_ref=recv.at[z_hi, there, source],
                         send_sem=adj_sem,
-                        recv_sem=recv_sem.at[z_hi],
+                        recv_sem=adj_recv_sem.at[z_hi],
                         device_id=(other, at_slab),
                         device_id_type=MESH,
                     ).start()
 
-                @pl.when(jnp.logical_not(remote))
-                def _():
-                    pltpu.make_async_copy(send.at[2 * b + c, plane], recv.at[z_hi, there, source], recv_sem.at[z_hi]).start()
+        @pl.when(itself)
+        def _():
+            mine = send.at[2 * my_block + z_hi, plane]
+            pltpu.make_async_copy(mine, recv.at[z_hi, there, source], adj_recv_sem.at[z_hi]).start()
 
     @pl.when(jnp.logical_not(work_inner))
     def _():
         recv[:, work] = jnp.zeros((2, 32, 8, LANES), jnp.bfloat16)
 
-    w_load.wait()
-    for height in range(2):
-        places = spread(height)
-        for i in range(3):
-
-            @pl.loop(0, 3)
-            def _(k):
-                at = pl.ds(pl.multiple_of(k * LANES, LANES), LANES)
-
-                @pl.when(z_hi == 0)
-                def _():
-                    left = jnp.concatenate([w_v[i, j, k] for j in range(3)], axis=1)
-                    total = jnp.dot(left, places, preferred_element_type=jnp.float32)
-                    taps[i, height, at, :] = total.astype(jnp.bfloat16)
-
-                @pl.when(z_hi == 1)
-                def _():
-                    left = jnp.concatenate([w_v[2 - i, 2 - j, 2 - k] for j in range(3)], axis=0)
-                    total = lax.dot_general(
-                        left, places, (((0,), (0,)), ((), ())), preferred_element_type=jnp.float32
-                    )
-                    taps[i, height, at, :] = total.astype(jnp.bfloat16)
-
-    for half in range(2):
+    @pl.when(z_hi == 1)
+    def _():
+        make_taps(True)
+
+    def side(half):
+        return pltpu.make_async_remote_copy(
+            src_ref=recv.at[half, 2 - core],
+            dst_ref=recv.at[half, 3 * core],
+            send_sem=side_send_sem.at[half],
+            recv_sem=side_recv_sem.at[half],
+            device_id=(beside, slab),
+            device_id_type=MESH,
+        )
+
+    def product(i, half, height):
+        right = jnp.concatenate([recv[half, i + p].reshape(256, LANES) for p in range(2)], axis=1)
+        return jnp.dot(taps[i, height, half], right, preferred_element_type=jnp.float32)
+
+    last = 2 - 2 * core
+    for turn in range(2):
+        half = z_hi if turn == 0 else 1 - z_hi
+        here = recv.at[half, pl.ds(1, 2)]
+        pltpu.make_async_copy(here, here, recv_sem.at[half]).wait()
+        side(half).start()
+        for height in range(2):
+            if turn == 0:
+                part_f[height] = product(1, half, height)
+            else:
+                part_f[height] += product(1, half, height)
 
         @pl.when(work_inner)
         def _():
-            here = recv.at[half, pl.ds(2 - work, 3)]
-            pltpu.make_async_copy(here, here, recv_sem.at[half]).wait()
-
-        @pl.when(jnp.logical_not(work_inner))
-        def _():
-            here = recv.at[half, pl.ds(1, 2)]
-            pltpu.make_async_copy(here, here, recv_sem.at[half]).wait()
-
-    side = pltpu.make_async_remote_copy(
-        src_ref=recv.at[:, 2 - core],
-        dst_ref=recv.at[:, 3 * core],
-        send_sem=side_send_sem,
-        recv_sem=side_recv_sem,
-        device_id=(beside, slab),
-        device_id_type=MESH,
-    )
-    side.start()
-
-    def right(i):
-        held = [[recv[half, i + p].reshape(256, LANES) for p in range(2)] for half in range(2)]
-        return jnp.concatenate([jnp.concatenate(planes, axis=1) for planes in held], axis=0)
-
-    last = 2 - 2 * core
-    for height in range(2):
-        part_f[height] = jnp.dot(
-            taps[1, height], right(1), preferred_element_type=jnp.float32
-        ) + jnp.dot(taps[2 - last, height], right(2 - last), preferred_element_type=jnp.float32)
-    side.wait_recv()
+            here = recv.at[half, 3 * core]
+            pltpu.make_async_copy(here, here, adj_recv_sem.at[half]).wait()
+
+        for height in range(2):
+            part_f[height] += product(2 - last, half, height)
+        side(half).wait_recv()
+        if turn == 0:
+            for height in range(2):
+                part_f[height] += product(last, half, height)
+
     col = lax.broadcasted_iota(jnp.int32, (LANES, LANES), 1)
     for height in range(2):
-        part = part_f[height] + jnp.dot(taps[last, height], right(last), preferred_element_type=jnp.float32)
+        part = part_f[height] + product(last, 1 - z_hi, height)
         for p in range(2):
             lanes = slice(LANES * p, LANES * (p + 1))
             before, here, after = (part[LANES * k : LANES * (k + 1), lanes] for k in range(3))
@@ -206,7 +215,8 @@
             ).start()
 
     pltpu.make_async_copy(landed, landed, out_recv_sem).wait()
-    side.wait_send()
+    for half in range(2):
+        side(half).wait_send()
     pltpu.make_async_copy(send, send, send_sem).wait()
 
     @pl.when(adj & jnp.logical_not(itself))
@@ -222,27 +232,35 @@
     pltpu.make_async_copy(out_send, out_send, out_send_sem).wait()
 
 
-def order_rows(landed, pre, grad, landed_f, rows_f):
-    for c, out in enumerate((pre, grad)):
-        landed_f[...] = landed[c].reshape(BLOCKS * 8, LANES).astype(jnp.float32)
+def order_rows(landed, pre, grad, landed_v, out_v, landed_f, rows_f, in_sem, out_sem):
+    loads = [pltpu.make_async_copy(landed.at[c], landed_v.at[c], in_sem.at[c]) for c in range(2)]
+    stores = [pltpu.make_async_copy(out_v.at[c], out, out_sem.at[c]) for c, out in enumerate((pre, grad))]
+    for load in loads:
+        load.start()
+    for c in range(2):
+        loads[c].wait()
+        landed_f[c] = landed_v[c].reshape(BLOCKS * 8, LANES).astype(jnp.float32)
         for ch in range(2):
             for p in range(2):
                 for height in range(2):
-                    rows_f[pl.ds(height, BLOCKS, stride=2), :] = landed_f[
-                        pl.ds(4 * p + 2 * height + ch, BLOCKS, stride=8), :
+                    rows_f[c, ch, p, pl.ds(height, BLOCKS, stride=2), :] = landed_f[
+                        c, pl.ds(4 * p + 2 * height + ch, BLOCKS, stride=8), :
                     ]
-                out[ch, p] = rows_f[...].astype(jnp.bfloat16)
+                out_v[c, ch, p] = rows_f[c, ch, p].astype(jnp.bfloat16)
+        stores[c].start()
+    for store in stores:
+        store.wait()
 
 
 def body(activations, cotangent, relu_mask, weights):
     bf16, f32 = jnp.bfloat16, jnp.float32
-    vmem, anywhere = pl.BlockSpec(memory_space=pltpu.VMEM), pl.BlockSpec(memory_space=pl.ANY)
+    anywhere = pl.BlockSpec(memory_space=pl.ANY)
     dma = pltpu.SemaphoreType.DMA
     landed = pl.pallas_call(
         kernel,
         out_shape=jax.ShapeDtypeStruct((2, BLOCKS, 8, LANES), bf16),
         in_specs=[anywhere] * 4,
-        out_specs=vmem,
+        out_specs=anywhere,
         scratch_shapes=[
             pltpu.VMEM((2, 2, 64, LANES), bf16),
             pltpu.VMEM((2, 2, 64, LANES), bf16),
@@ -251,7 +269,7 @@
             pltpu.VMEM((2, 2, 2, 80, LANES), f32),
             pltpu.VMEM((2 * BLOCKS, 2, 8, LANES), bf16),
             pltpu.VMEM((2, 4, 32, 8, LANES), bf16),
-            pltpu.VMEM((3, 2, 3 * LANES, 4 * LANES), bf16),
+            pltpu.VMEM((3, 2, 2, 3 * LANES, 2 * LANES), bf16),
             pltpu.VMEM((2, 3 * LANES, 2 * LANES), f32),
             pltpu.VMEM((2, 2, LANES, LANES), f32),
             pltpu.VMEM((64 * 8, LANES), f32),
@@ -261,8 +279,9 @@
             dma,
             dma,
             dma((2,)),
-            dma,
-            dma,
+            dma((2,)),
+            dma((2,)),
+            dma((2,)),
             dma,
             dma,
         ],
@@ -274,9 +293,17 @@
     return pl.pallas_call(
         order_rows,
         out_shape=(out, out),
-        in_specs=[vmem],
-        out_specs=(vmem, vmem),
-        scratch_shapes=[pltpu.VMEM((BLOCKS * 8, LANES), f32), pltpu.VMEM((64, LANES), f32)],
+        in_specs=[anywhere],
+        out_specs=(anywhere, anywhere),
+        scratch_shapes=[
+            pltpu.VMEM((2, BLOCKS, 8, LANES), bf16),
+            pltpu.VMEM((2, 2, 2, 64, LANES), bf16),
+            pltpu.VMEM((2, BLOCKS * 8, LANES), f32),
+            pltpu.VMEM((2, 2, 2, 64, LANES), f32),
+            dma((2,)),
+            dma((2,)),
+        ],
+        compiler_params=pltpu.CompilerParams(vmem_limit_bytes=63 * 1024 * 1024),
     )(landed)
 
 

time: 37.4 us -> 35.8 us (0.957)
  Pallas kernels: 36.7 us -> 35 us
    pallas_call x1, Pallas kernels: 35.1 us -> 33.4 us  [body(): pl.pallas_call(kernel, out_shape=jax.ShapeDtypeStruct((2, BLOCKS, 8, LANE...]
where the time goes in v3:
time: 35.8 us; the launch traced here: 35.6 us
  Pallas kernels  35 us (98%)
  between operations  0.64 us (2%)
    pallas_call x1, Pallas kernels, body(): pl.pallas_call(kernel, out_shape=jax.ShapeDtypeStruct((2, BLOCKS, 8, LANE...  33.4 us
    pallas_call x1, Pallas kernels, body(): pl.pallas_call(order_rows, out_shape=(out, out), in_specs=[anywhere], out...  1.61 us

profile of v3, /device:TPU:1, one launch (start us, length us, event | category | flops | bytes accessed | tf_op | source)
XLA Modules:
  0.0 35.6 jit_solution(11630467928528159657)
XLA Ops:
  0.6 33.4 %shard_map.59.landed = bf16[2,32,8,128]{3,2,1,0:T(8,128)(2,1)} custom-call(bf16[2,2,64,128]{3,2,1,0:T(8,128)(2,1)} %act.1, bf16[2,2,64,128]{3,2,1,0:T(8,128)(2,1)} %cot.1, s32[2,2,64,128]{3,2,1,0:T(8,128)} %mask.1, bf16[3,3,3,128,128]{4,3,2,1,0:T(8,128)(2,1)} %weights.1), custom_call_target="tpu_custom_call" | custom-call | tf_op jit(solution)/shard_map/pallas_call | solution.py:259
  34.0 1.6 %shard_map.60 = (bf16[2,2,64,128]{3,2,1,0:T(8,128)(2,1)}, bf16[2,2,64,128]{3,2,1,0:T(8,128)(2,1)}) custom-call(bf16[2,32,8,128]{3,2,1,0:T(8,128)(2,1)} %shard_map.59.landed), custom_call_target="tpu_custom_call" | custom-call | tf_op jit(solution)/shard_map/pallas_call | solution.py:293

commit v4 on v3

--- a/solution.py
+++ b/solution.py
@@ -43,23 +43,33 @@
         pltpu.make_async_copy(cot, cot_v, in_sem.at[1]),
         pltpu.make_async_copy(mask, mask_v, in_sem.at[2]),
     ]
-    for load in loads:
+    w_load = pltpu.make_async_copy(weights, w_v, w_sem)
+    barrier = pltpu.get_barrier_semaphore()
+
+    def greet(others, at_slab):
+        for other in others:
+            pl.semaphore_signal(barrier, inc=1, device_id=(other, at_slab), device_id_type=MESH)
+
+    for part in range(8):
+        others = range(8 * part, 8 * part + 8)
+        greet(others, work)
+
+        @pl.when(work_inner & ((work_adj != slab) | (chan // 8 != part)))
+        def _():
+            greet(others, work_adj)
+
+        @pl.when(work_inner & (work_adj == slab) & (chan // 8 == part))
+        def _():
+            for other in others:
+
+                @pl.when(other != chan)
+                def _():
+                    greet((other,), work_adj)
+
+    greet((beside,), slab)
+
+    for load in (*loads, w_load):
         load.start()
-    w_load = pltpu.make_async_copy(weights, w_v, w_sem)
-    w_load.start()
-
-    barrier = pltpu.get_barrier_semaphore()
-    pl.semaphore_signal(barrier, inc=1, device_id=(beside, slab), device_id_type=MESH)
-    for other in range(64):
-        pl.semaphore_signal(barrier, inc=1, device_id=(other, work), device_id_type=MESH)
-
-    @pl.when(work_inner)
-    def _():
-        @pl.loop(0, 64)
-        def _(other):
-            @pl.when((other != chan) | (work_adj != slab))
-            def _():
-                pl.semaphore_signal(barrier, inc=1, device_id=(other, work_adj), device_id_type=MESH)
 
     for load in loads:
         load.wait()
@@ -202,19 +212,26 @@
                 units_f[pl.ds(4 * p + 2 * height + ch, 64, stride=8), :] = rows_f[p, height, pl.ds(ch, 64, stride=2), :]
     out_send[...] = units_f[...].astype(jnp.bfloat16).reshape(64, 8, LANES)
 
+    def gate(half):
+        part = out_send.at[pl.ds(0, 32)]
+        pltpu.make_async_copy(part, part, out_send_sem.at[half]).wait()
+
     for half in range(2):
+        if half:
+            gate(0)
         for step in range(32):
             other = (step // 8) * 16 + half * 8 + step % 8
             pltpu.make_async_remote_copy(
                 src_ref=out_send.at[other],
                 dst_ref=landed.at[z_hi, my_block],
-                send_sem=out_send_sem,
+                send_sem=out_send_sem.at[half],
                 recv_sem=out_recv_sem,
                 device_id=(other, work),
                 device_id_type=MESH,
             ).start()
 
     pltpu.make_async_copy(landed, landed, out_recv_sem).wait()
+    gate(1)
     for half in range(2):
         side(half).wait_send()
     pltpu.make_async_copy(send, send, send_sem).wait()
@@ -228,8 +245,6 @@
     def _():
         sent = send.at[pl.ds(0, 63), 0]
         pltpu.make_async_copy(sent, sent, adj_sem).wait()
-
-    pltpu.make_async_copy(out_send, out_send, out_send_sem).wait()
 
 
 def order_rows(landed, pre, grad, landed_v, out_v, landed_f, rows_f, in_sem, out_sem):
@@ -282,7 +297,7 @@
             dma((2,)),
             dma((2,)),
             dma((2,)),
-            dma,
+            dma((2,)),
             dma,
         ],
         compiler_params=pltpu.CompilerParams(

time: 35.8 us -> 35.2 us (0.983)
  Pallas kernels: 35 us -> 34.5 us
    pallas_call x1, Pallas kernels: 33.4 us -> 32.8 us  [body(): pl.pallas_call(kernel, out_shape=jax.ShapeDtypeStruct((2, BLOCKS, 8, LANE...]
where the time goes in v4:
time: 35.2 us; the launch traced here: 35.1 us
  Pallas kernels  34.5 us (98%)
  between operations  0.64 us (2%)
    pallas_call x1, Pallas kernels, body(): pl.pallas_call(kernel, out_shape=jax.ShapeDtypeStruct((2, BLOCKS, 8, LANE...  32.8 us
    pallas_call x1, Pallas kernels, body(): pl.pallas_call(order_rows, out_shape=(out, out), in_specs=[anywhere], out...  1.61 us

profile of v4, /device:TPU:1, one launch (start us, length us, event | category | flops | bytes accessed | tf_op | source)
XLA Modules:
  0.0 35.1 jit_solution(18158521731497401458)
XLA Ops:
  0.6 32.8 %shard_map.59.landed = bf16[2,32,8,128]{3,2,1,0:T(8,128)(2,1)} custom-call(bf16[2,2,64,128]{3,2,1,0:T(8,128)(2,1)} %act.1, bf16[2,2,64,128]{3,2,1,0:T(8,128)(2,1)} %cot.1, s32[2,2,64,128]{3,2,1,0:T(8,128)} %mask.1, bf16[3,3,3,128,128]{4,3,2,1,0:T(8,128)(2,1)} %weights.1), custom_call_target="tpu_custom_call" | custom-call | tf_op jit(solution)/shard_map/pallas_call | solution.py:274
  33.5 1.6 %shard_map.60 = (bf16[2,2,64,128]{3,2,1,0:T(8,128)(2,1)}, bf16[2,2,64,128]{3,2,1,0:T(8,128)(2,1)}) custom-call(bf16[2,32,8,128]{3,2,1,0:T(8,128)(2,1)} %shard_map.59.landed), custom_call_target="tpu_custom_call" | custom-call | tf_op jit(solution)/shard_map/pallas_call | solution.py:308

commit v5 on v4

--- a/solution.py
+++ b/solution.py
@@ -8,6 +8,10 @@
 MESH = pl.DeviceIdType.MESH
 BLOCKS = 32
 LANES = 128
+FARTHEST_FIRST = sorted(
+    ((dx, dy) for dx in range(4) for dy in range(4)),
+    key=lambda d: (-min(d[0], 4 - d[0]) - min(d[1], 4 - d[1]), -min(d[0], 4 - d[0]), d),
+)
 
 
 def spread(height):
@@ -36,6 +40,9 @@
     work = 2 * (1 - slab // 2) + core
     work_inner = (work == 1) | (work == 2)
     work_adj = 3 - work
+    spots = []
+    for dx, dy in FARTHEST_FIRST:
+        spots.append(((chan // 16 + dx) % 4, (chan // 2 % 4 + dy) % 4))
     itself = adj & (core == slab - 1)
 
     loads = [
@@ -114,35 +121,34 @@
 
     pl.semaphore_wait(barrier, 65 + 64 * adj.astype(jnp.int32) - itself.astype(jnp.int32))
 
-    for c in (1, 0):
-        for b in range(BLOCKS):
-            pltpu.make_async_remote_copy(
-                src_ref=send.at[2 * b + c],
-                dst_ref=recv.at[z_hi, pl.ds(1, 2), source],
-                send_sem=send_sem,
-                recv_sem=recv_sem.at[z_hi],
-                device_id=((b // 8) * 16 + 8 * c + (b // 2 % 4) * 2 + slab % 2, 2 * (1 - pair) + b % 2),
-                device_id_type=MESH,
-            ).start()
+    for at_x, at_y, zb, c in [(*spot, zb, c) for spot in spots for c in (1, 0) for zb in range(2)]:
+        pltpu.make_async_remote_copy(
+            src_ref=send.at[16 * at_x + 4 * at_y + 2 * zb + c],
+            dst_ref=recv.at[z_hi, pl.ds(1, 2), source],
+            send_sem=send_sem,
+            recv_sem=recv_sem.at[z_hi],
+            device_id=(16 * at_x + 8 * c + 2 * at_y + slab % 2, 2 * (1 - pair) + zb),
+            device_id_type=MESH,
+        ).start()
 
     @pl.when(adj)
     def _():
         plane = 2 - slab
         there = 3 * (slab - 1)
-        for c in (1, 0):
-            for b in range(BLOCKS):
-                other, at_slab = (b // 8) * 16 + 8 * c + (b // 2 % 4) * 2 + slab - 1, 2 * pair + b % 2
-
-                @pl.when((other != chan) | (at_slab != slab))
-                def _():
-                    pltpu.make_async_remote_copy(
-                        src_ref=send.at[2 * b + c, plane],
-                        dst_ref=recv.at[z_hi, there, source],
-                        send_sem=adj_sem,
-                        recv_sem=adj_recv_sem.at[z_hi],
-                        device_id=(other, at_slab),
-                        device_id_type=MESH,
-                    ).start()
+        for at_x, at_y, zb, c in [(*spot, zb, c) for spot in spots for c in (1, 0) for zb in range(2)]:
+            unit = 16 * at_x + 4 * at_y + 2 * zb + c
+            other, at_slab = 16 * at_x + 8 * c + 2 * at_y + slab - 1, 2 * pair + zb
+
+            @pl.when((other != chan) | (at_slab != slab))
+            def _():
+                pltpu.make_async_remote_copy(
+                    src_ref=send.at[unit, plane],
+                    dst_ref=recv.at[z_hi, there, source],
+                    send_sem=adj_sem,
+                    recv_sem=adj_recv_sem.at[z_hi],
+                    device_id=(other, at_slab),
+                    device_id_type=MESH,
+                ).start()
 
         @pl.when(itself)
         def _():

time: 35.2 us -> 34.3 us (0.974)
  Pallas kernels: 34.5 us -> 33.5 us
    pallas_call x1, Pallas kernels: 32.8 us -> 31.9 us  [body(): pl.pallas_call(kernel, out_shape=jax.ShapeDtypeStruct((2, BLOCKS, 8, LANE...]
where the time goes in v5:
time: 34.3 us; the launch traced here: 34.2 us
  Pallas kernels  33.5 us (98%)
  between operations  0.64 us (2%)
    pallas_call x1, Pallas kernels, body(): pl.pallas_call(kernel, out_shape=jax.ShapeDtypeStruct((2, BLOCKS, 8, LANE...  31.9 us
    pallas_call x1, Pallas kernels, body(): pl.pallas_call(order_rows, out_shape=(out, out), in_specs=[anywhere], out...  1.61 us

profile of v5, /device:TPU:1, one launch (start us, length us, event | category | flops | bytes accessed | tf_op | source)
XLA Modules:
  0.0 34.2 jit_solution(7780008373923939333)
XLA Ops:
  0.6 31.9 %shard_map.59.landed = bf16[2,32,8,128]{3,2,1,0:T(8,128)(2,1)} custom-call(bf16[2,2,64,128]{3,2,1,0:T(8,128)(2,1)} %act.1, bf16[2,2,64,128]{3,2,1,0:T(8,128)(2,1)} %cot.1, s32[2,2,64,128]{3,2,1,0:T(8,128)} %mask.1, bf16[3,3,3,128,128]{4,3,2,1,0:T(8,128)(2,1)} %weights.1), custom_call_target="tpu_custom_call" | custom-call | tf_op jit(solution)/shard_map/pallas_call | solution.py:280
  32.6 1.6 %shard_map.60 = (bf16[2,2,64,128]{3,2,1,0:T(8,128)(2,1)}, bf16[2,2,64,128]{3,2,1,0:T(8,128)(2,1)}) custom-call(bf16[2,32,8,128]{3,2,1,0:T(8,128)(2,1)} %shard_map.59.landed), custom_call_target="tpu_custom_call" | custom-call | tf_op jit(solution)/shard_map/pallas_call | solution.py:314

commit v6 on v5

--- a/solution.py
+++ b/solution.py
@@ -226,7 +226,7 @@
         if half:
             gate(0)
         for step in range(32):
-            other = (step // 8) * 16 + half * 8 + step % 8
+            other = (step // 8) * 16 + half * 8 + (step % 8 + 1 - 2 * (step % 2))
             pltpu.make_async_remote_copy(
                 src_ref=out_send.at[other],
                 dst_ref=landed.at[z_hi, my_block],

time: 34.3 us -> 34.3 us (level)
  no operation moved by 1% of the time
where the time goes in v6:
time: 34.3 us; the launch traced here: 34.2 us
  Pallas kernels  33.5 us (98%)
  between operations  0.64 us (2%)
    pallas_call x1, Pallas kernels, body(): pl.pallas_call(kernel, out_shape=jax.ShapeDtypeStruct((2, BLOCKS, 8, LANE...  31.9 us
    pallas_call x1, Pallas kernels, body(): pl.pallas_call(order_rows, out_shape=(out, out), in_specs=[anywhere], out...  1.61 us

profile of v6, /device:TPU:1, one launch (start us, length us, event | category | flops | bytes accessed | tf_op | source)
XLA Modules:
  0.0 34.2 jit_solution(13978370309156198940)
XLA Ops:
  0.6 31.9 %shard_map.59.landed = bf16[2,32,8,128]{3,2,1,0:T(8,128)(2,1)} custom-call(bf16[2,2,64,128]{3,2,1,0:T(8,128)(2,1)} %act.1, bf16[2,2,64,128]{3,2,1,0:T(8,128)(2,1)} %cot.1, s32[2,2,64,128]{3,2,1,0:T(8,128)} %mask.1, bf16[3,3,3,128,128]{4,3,2,1,0:T(8,128)(2,1)} %weights.1), custom_call_target="tpu_custom_call" | custom-call | tf_op jit(solution)/shard_map/pallas_call | solution.py:280
  32.6 1.6 %shard_map.60 = (bf16[2,2,64,128]{3,2,1,0:T(8,128)(2,1)}, bf16[2,2,64,128]{3,2,1,0:T(8,128)(2,1)}) custom-call(bf16[2,32,8,128]{3,2,1,0:T(8,128)(2,1)} %shard_map.59.landed), custom_call_target="tpu_custom_call" | custom-call | tf_op jit(solution)/shard_map/pallas_call | solution.py:314
